TPU v7x, 256 devices: a whole 4x4x8 slice. The times are simulated.
256 devices in a mesh: seq: 16 (over z, core), wt: 16 (over x, y).
Axes of the slice: x: 4, y: 4, z: 8, core: 2. Of those that a mesh axis runs over, the one named last changes fastest.
Arguments:
- queries: bfloat16 [8192, 8192], P('seq', 'wt'), may hold values from -6 to 6
- keys_in: bfloat16 [8192, 8192], P('seq', 'wt'), may hold values from -6 to 6
- values_in: bfloat16 [8192, 8192], P('seq', 'wt'), may hold values from -6 to 6
- stream: bfloat16 [8192, 8192], P('seq', 'wt')
- attn_gain: float32 [8192], P('wt'), may hold values from 0.1 to 1.9
- mlp_gain: float32 [8192], replicated, may hold values from 0.1 to 1.9
- up_index: int32 [128, 16], P('wt'), may hold values from 0 to 63, all different within a row
- up_blocks: bfloat16 [128, 16, 128, 128], P('wt'), may hold values from -0.125 to 0.125
- down_index: int32 [128, 16], P('wt'), may hold values from 0 to 63, all different within a row
- down_blocks: bfloat16 [128, 16, 128, 128], P('wt'), may hold values from -0.09375 to 0.09375
Outputs:
- result: bfloat16 [8192, 8192], P('seq', 'wt')
Inputs may be any that keep to these rules, and one draw needn't show every extreme that they name: `up_index`: each row names 16 different feature blocks, and every feature block is named by some row. `down_index`: each row names 16 different output blocks, and every output block is named by some row.
All inputs are finite; a program needn't handle non-finite values.
Results may differ from a plain program's by a relative error of at most 0.013.
Values may be sent and summed in bfloat16 or wider, within the bound.
No kernel may reach another device: no remote copies, remote signals or barrier semaphores. Data moves between devices by JAX's collectives and lax.ppermute only.
A program may use at most 128 MiB of HBM per device.

v0:
```python
import jax
import jax.numpy as jnp
from jax import lax
from jax.sharding import PartitionSpec as P

HEAD = 128
BLK = 128


def carried_in(x, axis, join, neutral):
    place = lax.axis_index(axis)
    gathered = lax.all_gather(x.astype(jnp.bfloat16), axis)
    state = jnp.zeros_like(x) + jnp.asarray(neutral, x.dtype)

    def one(step, state):
        return join(state, lax.dynamic_index_in_dim(gathered, step, 0, False).astype(x.dtype))

    return lax.fori_loop(0, place, one, state)


def feature_map(a):
    return (jax.nn.elu(a.astype(jnp.float32)) + 1.0).astype(jnp.bfloat16)


def add_states(earlier, later):
    return earlier + later


def per_device(
    queries,
    keys_in,
    values_in,
    stream,
    attn_gain,
    mlp_gain,
    up_index,
    up_blocks,
    down_index,
    down_blocks,
):
    rows = queries.shape[0]
    local_cols = queries.shape[1]
    local_heads = local_cols // HEAD
    fq = feature_map(queries).reshape(rows, local_heads, HEAD)
    fk = feature_map(keys_in).reshape(rows, local_heads, HEAD)
    vals = values_in.reshape(rows, local_heads, HEAD)
    causal = jnp.tril(jnp.ones((rows, rows), dtype=bool))
    scores = jnp.einsum("thd,shd->hts", fq, fk, preferred_element_type=jnp.float32)
    scores = jnp.where(causal[None], scores, 0.0).astype(jnp.bfloat16)
    intra = jnp.einsum("hts,shd->thd", scores, vals, preferred_element_type=jnp.float32)
    own_state = jnp.einsum("shd,she->hde", fk, vals, preferred_element_type=jnp.float32)
    empty = jnp.zeros_like(own_state)
    before = carried_in(own_state, "seq", add_states, empty)
    inter = jnp.einsum(
        "thd,hde->the", fq.astype(jnp.float32), before, precision=lax.Precision.HIGHEST
    )
    raw = intra + inter
    normal_raw = raw * lax.rsqrt(jnp.mean(raw * raw, axis=-1, keepdims=True) + 1e-06)
    attn = normal_raw.reshape(rows, local_cols) * attn_gain
    mid = (stream.astype(jnp.float32) + attn).astype(jnp.bfloat16)
    width = mlp_gain.shape[0]
    whole = lax.all_gather(mid, "wt", axis=1, tiled=True)
    whole_f = whole.astype(jnp.float32)
    scale = lax.rsqrt(jnp.mean(whole_f * whole_f, axis=-1, keepdims=True) + 1e-06)
    normed = (whole_f * scale * mlp_gain).astype(jnp.bfloat16)
    tiles = normed.reshape(rows, width // BLK, BLK)
    own_blocks = up_blocks.shape[0]
    picks = jnp.take(tiles, up_index.reshape(-1), axis=1)
    picks = picks.reshape(rows, own_blocks, up_index.shape[1], BLK)
    upper = jnp.einsum("lckd,ckde->lce", picks, up_blocks, preferred_element_type=jnp.float32)
    act = jax.nn.silu(upper).astype(jnp.bfloat16)
    parts = jnp.einsum("lrd,rkde->rkle", act, down_blocks, preferred_element_type=jnp.float32)
    parts = parts.reshape(-1, rows, BLK)
    summed = jax.ops.segment_sum(parts, down_index.reshape(-1), num_segments=width // BLK)
    partial_sum = summed.astype(jnp.bfloat16)
    mine = lax.psum_scatter(partial_sum, "wt", scatter_dimension=0, tiled=True).astype(jnp.float32)
    down = jnp.transpose(mine, (1, 0, 2)).reshape(rows, local_cols)
    return (mid.astype(jnp.float32) + down).astype(jnp.bfloat16)


def solution(mesh):
    placed = (
        P("seq", "wt"),
        P("seq", "wt"),
        P("seq", "wt"),
        P("seq", "wt"),
        P("wt"),
        P(),
        P("wt", None),
        P("wt", None, None, None),
        P("wt", None),
        P("wt", None, None, None),
    )
    return jax.shard_map(
        per_device, mesh=mesh, in_specs=placed, out_specs=P("seq", "wt"), check_vma=False
    )
```

profile of v0, /device:TPU:2, one launch (start us, length us, event | category | flops | bytes accessed | tf_op | source)
XLA Modules:
  0.0 391.9 jit_solution(10710767317259980740)
XLA Ops:
  6.5 1.6 fusion.27
  8.1 0.2 copy.49
  8.4 0.9 convolution_convert_fusion
  9.3 0.0 all-gather.6.cloned.1.call-update
  9.3 0.0 all-gather.4.cloned.1.call-start
  9.4 1.3 copy.35
  10.7 0.1 iota_compare_fusion
  10.7 41.4 %all-gather.6.cloned.1.call-done = bf16[64,128,128]{2,1,0:T(8,128)(2,1)} async-done(((bf16[4,128,128]{2,1,0:T(8,128)(2,1)}), bf16[64,128,128]{2,1,0:T(8,128)(2,1)}) %all-gather.6.cloned.1.call-update) | async-done | bytes 2097168 | tf_op jit(solution)/shard_map/all_gather | solution.py:12
  52.2 1.9 convolution_bitcast_fusion
  54.2 2.8 multiply_reduce_fusion
  57.1 0.1 broadcast_multiply_fusion
  57.2 1.0 fusion.30
  58.2 0.0 all-gather.4.cloned.1.call-update
  58.2 0.2 reduce-scatter.2.cloned.1.call-start
  58.5 0.1 reshape.114
  58.6 0.1 reshape.96
  58.7 87.3 %all-gather.4.cloned.1.call-done = bf16[512,8192]{0,1:T(8,128)(2,1)} async-done(((bf16[512,512]{0,1:T(8,128)(2,1)}), bf16[512,8192]{0,1:T(8,128)(2,1)}) %all-gather.4.cloned.1.call-update) | async-done | bytes 8388624 | tf_op jit(solution)/shard_map/all_gather | solution.py:62
  146.0 5.3 %fusion = f32[512]{0:T(512)S(1)} fusion(bf16[512,8192]{0,1:T(8,128)(2,1)} %all-gather.4.cloned.1.call-done), kind=kLoop, calls=%fused_computation.5 | loop fusion | flops 12582400 | bytes 8390656 | tf_op jit(solution)/shard_map/reduce_sum | solution.py:64
  151.3 0.4 copy-done.2
  151.7 4.4 %fusion.2 = bf16[512,8192]{0,1:T(8,128)(2,1)} fusion(bf16[512,8192]{0,1:T(8,128)(2,1)S(1)} %copy-done.2, f32[8192]{0:T(1024)S(1)} %copy-done.4, f32[512]{0:T(512)S(1)} %add_rsqrt_fusion.1), kind=kLoop, calls=%fused_computation.7 | loop fusion | flops 16777216 | bytes 16812032 | tf_op jit(solution)/shard_map/convert_element_type | solution.py:65
  156.1 12.0 %copy.43 = bf16[512,64,128]{2,0,1:T(8,128)(2,1)} copy(bf16[512,64,128]{0,2,1:T(8,128)(2,1)} %bitcast.96) | data formatting | bytes 16777216 | tf_op jit(solution)/shard_map/reshape | solution.py:66
  168.1 11.8 %gather_fusion = bf16[128,512,128]{2,1,0:T(8,128)(2,1)} fusion(bf16[512,64,128]{2,0,1:T(8,128)(2,1)} %copy.43, s32[1024]{0:T(1024)S(1)} %pad_clamp_fusion), kind=kCustom, calls=%fused_computation | custom fusion | bytes 33554944 | tf_op jit(solution)/shard_map/jit(_take)/gather | solution.py:68
  179.9 21.8 %fusion.20 = f32[8,512,16,128]{3,1,2,0:T(8,128)} fusion(bf16[8,16,128,128]{3,2,1,0:T(8,128)(2,1)} %param.21, bf16[8,16,128,128]{3,2,1,0:T(8,128)(2,1)} %param.19, bf16[512,8,16,128]{3,0,2,1:T(8,128)(2,1)} %bitcast.95, pred[8,16]{1,0:T(8,128)(4,1)S(1)} %compare_and_fusion), kind=kOutput, calls=%fused_computation.28 | convolution fusion | flops 4305977344 | bytes 58720384 | tf_op jit(solution)/shard_map/lrd,rkde->rkle/dot_general | solution.py:72
  201.7 7.8 %broadcast_in_dim.43 = f32[64,512,128]{2,1,0:T(8,128)} broadcast(f32[]{:T(128)} %constant.27.clone.1), dimensions={} | broadcast | bytes 16777220 | tf_op jit(solution)/shard_map/broadcast_in_dim | solution.py:74
  209.5 73.8 %scatter_fusion = f32[64,512,128]{2,1,0:T(8,128)} fusion(f32[64,512,128]{2,1,0:T(8,128)} %broadcast_in_dim.43, s32[128]{0:T(128)S(1)} %reshape.114, f32[128,512,128]{2,1,0:T(8,128)} %bitcast.94), kind=kCustom, calls=%fused_computation.1 | custom fusion | flops 8388608 | bytes 100663808 | tf_op jit(solution)/shard_map/scatter-add | solution.py:74
  283.3 9.3 %convert_element_type.62 = bf16[64,512,128]{2,1,0:T(8,128)(2,1)} convert(f32[64,512,128]{2,1,0:T(8,128)} %scatter_fusion) | non-fusion elementwise | flops 4194304 | bytes 25165824 | tf_op jit(solution)/shard_map/convert_element_type | solution.py:75
  292.6 0.0 reduce-scatter.2.cloned.1.call-update
  292.6 90.1 %reduce-scatter.2.cloned.1.call-done = bf16[4,512,128]{2,1,0:T(8,128)(2,1)} async-done(((bf16[64,512,128]{2,1,0:T(8,128)(2,1)}), bf16[4,512,128]{2,1,0:T(8,128)(2,1)}) %reduce-scatter.2.cloned.1.call-update) | async-done | bytes 524304 | tf_op jit(solution)/shard_map/reduce_scatter | solution.py:76
  382.7 1.1 convert_bitcast_fusion
  383.8 0.3 copy.44
  384.2 0.2 fusion.28
  384.4 1.0 copy.45
  (25 shorter events, 0.1 us)
Async XLA Ops:
  6.5 1.8 copy-start
  6.5 45.7 %copy-start.8 = (bf16[512,512]{1,0:T(8,128)(2,1)S(1)}, bf16[512,512]{1,0:T(8,128)(2,1)}, u32[]{:S(2)}) copy-start(bf16[512,512]{1,0:T(8,128)(2,1)} %param.12) | copy-start | bytes 1572868
  6.5 45.6 %all-gather.6.cloned.1.call-start = ((), (), s32[]{:S(2)}) async-start(), calls=%async_computation.3 | async-start | bytes 2228224 | tf_op jit(solution)/shard_map/all_gather | solution.py:12
  9.3 136.6 %all-gather.4.cloned.1.call-start = ((), (), s32[]{:S(2)}) async-start(), calls=%async_computation.1 | async-start | bytes 8912896 | tf_op jit(solution)/shard_map/all_gather | solution.py:62
  10.6 46.6 %copy-start.7 = (f32[512]{0:T(512)S(1)}, f32[512]{0:T(512)}, u32[]{:S(2)}) copy-start(f32[512]{0:T(512)} %param.16) | copy-start | bytes 6148
  52.2 6.3 %copy-start.6 = (s32[8,16]{1,0:T(8,128)S(1)}, s32[8,16]{1,0:T(8,128)}, u32[]{:S(2)}) copy-start(s32[8,16]{1,0:T(8,128)} %param.20) | copy-start | bytes 1540
  52.2 6.3 %copy-start.5 = (s32[8,16]{1,0:T(8,128)S(1)}, s32[8,16]{1,0:T(8,128)}, u32[]{:S(2)}) copy-start(s32[8,16]{1,0:T(8,128)} %param.18) | copy-start | bytes 1540
  57.0 94.2 %copy-start.4 = (f32[8192]{0:T(1024)S(1)}, f32[8192]{0:T(1024)}, u32[]{:S(2)}) copy-start(f32[8192]{0:T(1024)} %param.17) | copy-start | bytes 98308
  58.2 324.5 %reduce-scatter.2.cloned.1.call-start = ((), (), s32[]{:S(2)}) async-start(), calls=%async_computation.2 | async-start | bytes 8912896 | tf_op jit(solution)/shard_map/reduce_scatter | solution.py:76
  146.0 5.8 %copy-start.2 = (bf16[512,8192]{0,1:T(8,128)(2,1)S(1)}, bf16[512,8192]{0,1:T(8,128)(2,1)}, u32[]{:S(2)}) copy-start(bf16[512,8192]{0,1:T(8,128)(2,1)} %all-gather.4.cloned.1.call-done) | copy-start | bytes 25165828
  283.3 102.1 %copy-start.1 = (bf16[512,512]{1,0:T(8,128)(2,1)S(1)}, bf16[512,512]{1,0:T(8,128)(2,1)}, u32[]{:S(2)}) copy-start(bf16[512,512]{1,0:T(8,128)(2,1)} %param.14) | copy-start | bytes 1572868
  292.6 91.6 %copy-start.3 = (bf16[512,512]{0,1:T(8,128)(2,1)S(1)}, bf16[512,512]{0,1:T(8,128)(2,1)}, u32[]{:S(2)}) copy-start(bf16[512,512]{0,1:T(8,128)(2,1)} %fusion.30) | copy-start | bytes 1572868
Sparse Core Ops, SparseCore 0:
  9.5 42.6 all-gather.5
  58.4 87.5 all-gather.3
  292.7 89.9 reduce-scatter.1
where the time goes:
time: 393 us; the launch traced here: 392 us
  waiting for transfers between devices  219 us (56%)
  other arithmetic  96.8 us (25%)
  local copies, waits for them, and re-layouts  35.1 us (9%)
  matrix products  27.6 us (7%)
  between operations  13.3 us (3%)
    reduce_scatter x1, waiting for transfers between devices, per_device(): lax.psum_scatter(partial_sum, 'wt', scatter_dimension=0, tiled=True)  90.1 us
    all_gather x1, waiting for transfers between devices, per_device(): whole = lax.all_gather(mid, 'wt', axis=1, tiled=True)  87.3 us
    scatter-add x1, other arithmetic, per_device(): jax.ops.segment_sum(parts, down_index.reshape(-1), num_segments=width //...  73.8 us
    all_gather x1, waiting for transfers between devices, carried_in(): gathered = lax.all_gather(x.astype(jnp.bfloat16), axis)  41.4 us
    dot_general x1, matrix products, per_device(): jnp.einsum('lrd,rkde->rkle', act, down_blocks, preferred_element_type=jnp...  21.8 us
    reshape x1, local copies, waits for them, and re-layouts, per_device(): tiles = normed.reshape(rows, width // BLK, BLK)  12 us
    gather x1, local copies, waits for them, and re-layouts, per_device(): picks = jnp.take(tiles, up_index.reshape(-1), axis=1)  11.8 us
    convert_element_type x1, other arithmetic, per_device(): partial_sum = summed.astype(jnp.bfloat16)  9.25 us
  transfers between devices with their start and end apart: 3, of which 3 were waited for; matrix products, arithmetic and copies ran while one was open for 0% of the time, Pallas kernels for 0%

commit v1 on v0

--- a/solution.py
+++ b/solution.py
@@ -59,7 +59,14 @@
     attn = normal_raw.reshape(rows, local_cols) * attn_gain
     mid = (stream.astype(jnp.float32) + attn).astype(jnp.bfloat16)
     width = mlp_gain.shape[0]
-    whole = lax.all_gather(mid, "wt", axis=1, tiled=True)
+    count = lax.axis_size("wt")
+    forward = [(i, (i + 1) % count) for i in range(count)]
+    shards = [mid]
+    for stride in range(1, count):
+        shards = [lax.ppermute(shards[0], "wt", forward), *shards]
+    result = jnp.concatenate(shards, axis=1)
+    turn = (lax.axis_index("wt") + 1) * shards[-1].shape[1]
+    whole = jnp.roll(result, turn, axis=1)
     whole_f = whole.astype(jnp.float32)
     scale = lax.rsqrt(jnp.mean(whole_f * whole_f, axis=-1, keepdims=True) + 1e-06)
     normed = (whole_f * scale * mlp_gain).astype(jnp.bfloat16)

time: 393 us -> 556 us (1.41)
  waiting for transfers between devices: 219 us -> 365 us
  local copies, waits for them, and re-layouts: 35.1 us -> 52.8 us
    ppermute x0 -> x15, waiting for transfers between devices: none -> 212 us  [per_device(): shards = [lax.ppermute(shards[0], 'wt', forward), *shards]]
    all_gather x1 -> x0, waiting for transfers between devices: 87.3 us -> none  [per_device(): whole = lax.all_gather(mid, 'wt', axis=1, tiled=True)]
    reduce_scatter x1, waiting for transfers between devices: 90.1 us -> 111 us  [per_device(): lax.psum_scatter(partial_sum, 'wt', scatter_dimension=0, tiled=True)]
    unnamed x19 -> x72, local copies, waits for them, and re-layouts: 1.74 us -> 19.5 us
  transfers between devices with their start and end apart: 3 -> 17, of which waited for: 3 -> 17; matrix products, arithmetic and copies ran while one was open for 0% -> 0% of each run, Pallas kernels for 0% -> 0%
where the time goes in v1:
time: 556 us; the launch traced here: 554 us
  waiting for transfers between devices  365 us (66%)
  other arithmetic  92.3 us (17%)
  local copies, waits for them, and re-layouts  52.8 us (9%)
  matrix products  28.6 us (5%)
  between operations  13.9 us (2%)
    ppermute x15, waiting for transfers between devices, per_device(): shards = [lax.ppermute(shards[0], 'wt', forward), *shards]  212 us
    reduce_scatter x1, waiting for transfers between devices, per_device(): lax.psum_scatter(partial_sum, 'wt', scatter_dimension=0, tiled=True)  111 us
    scatter-add x1, other arithmetic, per_device(): jax.ops.segment_sum(parts, down_index.reshape(-1), num_segments=width //...  73.6 us
    all_gather x1, waiting for transfers between devices, carried_in(): gathered = lax.all_gather(x.astype(jnp.bfloat16), axis)  41.4 us
    dot_general x1, matrix products, per_device(): jnp.einsum('lrd,rkde->rkle', act, down_blocks, preferred_element_type=jnp...  21.8 us
    unnamed x72, local copies, waits for them, and re-layouts  19.5 us
    reshape x1, local copies, waits for them, and re-layouts, per_device(): tiles = normed.reshape(rows, width // BLK, BLK)  12 us
    gather x1, local copies, waits for them, and re-layouts, per_device(): picks = jnp.take(tiles, up_index.reshape(-1), axis=1)  11.8 us
  transfers between devices with their start and end apart: 17, of which 17 were waited for; matrix products, arithmetic and copies ran while one was open for 0% of the time, Pallas kernels for 0%

profile of v1, /device:TPU:2, one launch (start us, length us, event | category | flops | bytes accessed | tf_op | source)
XLA Modules:
  0.0 554.1 jit_solution(6549811507403211026)
XLA Ops:
  6.6 1.6 fusion.27
  9.4 1.3 copy.35
  10.7 41.4 %all-gather.3.cloned.1.call-done = bf16[64,128,128]{2,1,0:T(8,128)(2,1)} async-done(((bf16[4,128,128]{2,1,0:T(8,128)(2,1)}), bf16[64,128,128]{2,1,0:T(8,128)(2,1)}) %all-gather.3.cloned.1.call-update) | async-done | bytes 2097168 | tf_op jit(solution)/shard_map/all_gather | solution.py:12
  52.2 3.0 convolution_bitcast_fusion
  55.2 2.8 multiply_reduce_fusion
  58.4 1.6 collective-permute-start
  60.0 15.2 %collective-permute-done = bf16[512,512]{0,1:T(8,128)(2,1)S(1)} collective-permute-done((bf16[512,512]{0,1:T(8,128)(2,1)S(1)}, bf16[512,512]{0,1:T(8,128)(2,1)S(1)}, u32[]{:S(2)}, u32[]{:S(2)}) %collective-permute-start) | collective-permute-done | bytes 524320 | tf_op jit(solution)/shard_map/ppermute | solution.py:66
  75.2 16.1 %collective-permute-done.1 = bf16[512,512]{0,1:T(8,128)(2,1)S(1)} collective-permute-done((bf16[512,512]{0,1:T(8,128)(2,1)S(1)}, bf16[512,512]{0,1:T(8,128)(2,1)S(1)}, u32[]{:S(2)}, u32[]{:S(2)}) %collective-permute-start.1) | collective-permute-done | bytes 524320 | tf_op jit(solution)/shard_map/ppermute | solution.py:66
  91.2 15.2 %collective-permute-done.2 = bf16[512,512]{0,1:T(8,128)(2,1)S(1)} collective-permute-done((bf16[512,512]{0,1:T(8,128)(2,1)S(1)}, bf16[512,512]{0,1:T(8,128)(2,1)S(1)}, u32[]{:S(2)}, u32[]{:S(2)}) %collective-permute-start.2) | collective-permute-done | bytes 524320 | tf_op jit(solution)/shard_map/ppermute | solution.py:66
  106.4 14.3 %collective-permute-done.3 = bf16[512,512]{0,1:T(8,128)(2,1)S(1)} collective-permute-done((bf16[512,512]{0,1:T(8,128)(2,1)S(1)}, bf16[512,512]{0,1:T(8,128)(2,1)S(1)}, u32[]{:S(2)}, u32[]{:S(2)}) %collective-permute-start.3) | collective-permute-done | bytes 524320 | tf_op jit(solution)/shard_map/ppermute | solution.py:66
  120.7 13.4 %collective-permute-done.4 = bf16[512,512]{0,1:T(8,128)(2,1)S(1)} collective-permute-done((bf16[512,512]{0,1:T(8,128)(2,1)S(1)}, bf16[512,512]{0,1:T(8,128)(2,1)S(1)}, u32[]{:S(2)}, u32[]{:S(2)}) %collective-permute-start.4) | collective-permute-done | bytes 524320 | tf_op jit(solution)/shard_map/ppermute | solution.py:66
  134.1 12.5 %collective-permute-done.5 = bf16[512,512]{0,1:T(8,128)(2,1)S(1)} collective-permute-done((bf16[512,512]{0,1:T(8,128)(2,1)S(1)}, bf16[512,512]{0,1:T(8,128)(2,1)S(1)}, u32[]{:S(2)}, u32[]{:S(2)}) %collective-permute-start.5) | collective-permute-done | bytes 524320 | tf_op jit(solution)/shard_map/ppermute | solution.py:66
  147.4 11.5 %collective-permute-done.6 = bf16[512,512]{0,1:T(8,128)(2,1)S(1)} collective-permute-done((bf16[512,512]{0,1:T(8,128)(2,1)S(1)}, bf16[512,512]{0,1:T(8,128)(2,1)S(1)}, u32[]{:S(2)}, u32[]{:S(2)}) %collective-permute-start.6) | collective-permute-done | bytes 524320 | tf_op jit(solution)/shard_map/ppermute | solution.py:66
  159.7 12.2 %collective-permute-done.7 = bf16[512,512]{0,1:T(8,128)(2,1)S(1)} collective-permute-done((bf16[512,512]{0,1:T(8,128)(2,1)S(1)}, bf16[512,512]{0,1:T(8,128)(2,1)S(1)}, u32[]{:S(2)}, u32[]{:S(2)}) %collective-permute-start.7) | collective-permute-done | bytes 524320 | tf_op jit(solution)/shard_map/ppermute | solution.py:66
  172.7 13.3 %collective-permute-done.8 = bf16[512,512]{0,1:T(8,128)(2,1)S(1)} collective-permute-done((bf16[512,512]{0,1:T(8,128)(2,1)S(1)}, bf16[512,512]{0,1:T(8,128)(2,1)S(1)}, u32[]{:S(2)}, u32[]{:S(2)}) %collective-permute-start.8) | collective-permute-done | bytes 524320 | tf_op jit(solution)/shard_map/ppermute | solution.py:66
  186.8 14.3 %collective-permute-done.9 = bf16[512,512]{0,1:T(8,128)(2,1)S(1)} collective-permute-done((bf16[512,512]{0,1:T(8,128)(2,1)S(1)}, bf16[512,512]{0,1:T(8,128)(2,1)S(1)}, u32[]{:S(2)}, u32[]{:S(2)}) %collective-permute-start.9) | collective-permute-done | bytes 524320 | tf_op jit(solution)/shard_map/ppermute | solution.py:66
  202.0 15.5 %collective-permute-done.10 = bf16[512,512]{0,1:T(8,128)(2,1)S(1)} collective-permute-done((bf16[512,512]{0,1:T(8,128)(2,1)S(1)}, bf16[512,512]{0,1:T(8,128)(2,1)S(1)}, u32[]{:S(2)}, u32[]{:S(2)}) %collective-permute-start.10) | collective-permute-done | bytes 524320 | tf_op jit(solution)/shard_map/ppermute | solution.py:66
  218.2 16.6 %collective-permute-done.11 = bf16[512,512]{0,1:T(8,128)(2,1)S(1)} collective-permute-done((bf16[512,512]{0,1:T(8,128)(2,1)S(1)}, bf16[512,512]{0,1:T(8,128)(2,1)S(1)}, u32[]{:S(2)}, u32[]{:S(2)}) %collective-permute-start.11) | collective-permute-done | bytes 524320 | tf_op jit(solution)/shard_map/ppermute | solution.py:66
  235.6 15.7 %collective-permute-done.12 = bf16[512,512]{0,1:T(8,128)(2,1)} collective-permute-done((bf16[512,512]{0,1:T(8,128)(2,1)S(1)}, bf16[512,512]{0,1:T(8,128)(2,1)}, u32[]{:S(2)}, u32[]{:S(2)}) %collective-permute-start.12) | collective-permute-done | bytes 524320 | tf_op jit(solution)/shard_map/ppermute | solution.py:66
  251.5 14.8 %collective-permute-done.13 = bf16[512,512]{0,1:T(8,128)(2,1)} collective-permute-done((bf16[512,512]{0,1:T(8,128)(2,1)}, bf16[512,512]{0,1:T(8,128)(2,1)}, u32[]{:S(2)}, u32[]{:S(2)}) %collective-permute-start.13) | collective-permute-done | bytes 524320 | tf_op jit(solution)/shard_map/ppermute | solution.py:66
  266.3 11.5 %collective-permute-done.14 = bf16[512,512]{0,1:T(8,128)(2,1)S(1)} collective-permute-done((bf16[512,512]{0,1:T(8,128)(2,1)}, bf16[512,512]{0,1:T(8,128)(2,1)S(1)}, u32[]{:S(2)}, u32[]{:S(2)}) %collective-permute-start.14) | collective-permute-done | bytes 524320 | tf_op jit(solution)/shard_map/ppermute | solution.py:66
  285.4 1.1 constant_dynamic-update-slice_fusion.23
  290.7 1.8 fusion
  292.5 4.4 fusion.2
  296.9 12.0 %copy.43 = bf16[512,64,128]{2,0,1:T(8,128)(2,1)} copy(bf16[512,64,128]{0,2,1:T(8,128)(2,1)} %bitcast.96) | data formatting | bytes 16777216 | tf_op jit(solution)/shard_map/reshape | solution.py:73
  308.9 11.8 %gather_fusion = bf16[128,512,128]{2,1,0:T(8,128)(2,1)} fusion(bf16[512,64,128]{2,0,1:T(8,128)(2,1)} %copy.43, s32[1024]{0:T(1024)S(1)} %pad_clamp_fusion), kind=kCustom, calls=%fused_computation | custom fusion | bytes 33554944 | tf_op jit(solution)/shard_map/jit(_take)/gather | solution.py:75
  320.7 21.8 %fusion.20 = f32[8,512,16,128]{3,1,2,0:T(8,128)} fusion(bf16[8,16,128,128]{3,2,1,0:T(8,128)(2,1)} %param.21, bf16[8,16,128,128]{3,2,1,0:T(8,128)(2,1)} %param.19, bf16[512,8,16,128]{3,0,2,1:T(8,128)(2,1)} %bitcast.95, pred[8,16]{1,0:T(8,128)(4,1)S(1)} %compare_and_fusion), kind=kOutput, calls=%fused_computation.28 | convolution fusion | flops 4305977344 | bytes 58720384 | tf_op jit(solution)/shard_map/lrd,rkde->rkle/dot_general | solution.py:79
  342.5 7.8 %broadcast_in_dim.43 = f32[64,512,128]{2,1,0:T(8,128)} broadcast(f32[]{:T(128)} %constant.67.clone.1), dimensions={} | broadcast | bytes 16777220 | tf_op jit(solution)/shard_map/broadcast_in_dim | solution.py:81
  350.3 73.6 %scatter_fusion = f32[64,512,128]{2,1,0:T(8,128)} fusion(f32[64,512,128]{2,1,0:T(8,128)} %broadcast_in_dim.43, s32[128]{0:T(128)S(1)} %reshape.114, f32[128,512,128]{2,1,0:T(8,128)} %bitcast.94), kind=kCustom, calls=%fused_computation.1 | custom fusion | flops 8388608 | bytes 100663808 | tf_op jit(solution)/shard_map/scatter-add | solution.py:81
  423.9 9.2 %convert_element_type.62 = bf16[64,512,128]{2,1,0:T(8,128)(2,1)} convert(f32[64,512,128]{2,1,0:T(8,128)} %scatter_fusion) | non-fusion elementwise | flops 4194304 | bytes 25165824 | tf_op jit(solution)/shard_map/convert_element_type | solution.py:82
  433.2 111.4 %reduce-scatter.2.cloned.1.call-done = bf16[4,512,128]{2,1,0:T(8,128)(2,1)} async-done(((bf16[64,512,128]{2,1,0:T(8,128)(2,1)}), bf16[4,512,128]{2,1,0:T(8,128)(2,1)}) %reduce-scatter.2.cloned.1.call-update) | async-done | bytes 524304 | tf_op jit(solution)/shard_map/reduce_scatter | solution.py:83
  544.6 1.1 convert_bitcast_fusion
  (106 shorter events, 20.7 us)
Async XLA Ops:
  6.5 1.8 copy-start
  6.5 51.7 %copy-start.19 = (f32[512]{0:T(512)S(1)}, f32[512]{0:T(512)}, u32[]{:S(2)}) copy-start(f32[512]{0:T(512)} %param.16) | copy-start | bytes 6148
  6.5 244.8 %copy-start.18 = (s32[8,16]{1,0:T(8,128)S(1)}, s32[8,16]{1,0:T(8,128)}, u32[]{:S(2)}) copy-start(s32[8,16]{1,0:T(8,128)} %param.20) | copy-start | bytes 1540
  6.5 244.8 %copy-start.17 = (s32[8,16]{1,0:T(8,128)S(1)}, s32[8,16]{1,0:T(8,128)}, u32[]{:S(2)}) copy-start(s32[8,16]{1,0:T(8,128)} %param.18) | copy-start | bytes 1540
  6.5 45.6 %all-gather.3.cloned.1.call-start = ((), (), s32[]{:S(2)}) async-start(), calls=%async_computation.2 | async-start | bytes 2228224 | tf_op jit(solution)/shard_map/all_gather | solution.py:12
  9.3 535.3 %reduce-scatter.2.cloned.1.call-start = ((), (), s32[]{:S(2)}) async-start(), calls=%async_computation.1 | async-start | bytes 8912896 | tf_op jit(solution)/shard_map/reduce_scatter | solution.py:83
  58.4 16.7 %collective-permute-start = (bf16[512,512]{0,1:T(8,128)(2,1)S(1)}, bf16[512,512]{0,1:T(8,128)(2,1)S(1)}, u32[]{:S(2)}, u32[]{:S(2)}) collective-permute-start(bf16[512,512]{0,1:T(8,128)(2,1)S(1)} %fusion.30), channel_id=1, source_target_pairs={{0,1},{1,2},{2,3},{3,4},{4,5},{5,6},{6,7},{7,8},{8,9},{9,10},{10,1... | collective-permute-start | bytes 1572872 | tf_op jit(solution)/shard_map/ppermute | solution.py:66
  75.2 16.1 %collective-permute-start.1 = (bf16[512,512]{0,1:T(8,128)(2,1)S(1)}, bf16[512,512]{0,1:T(8,128)(2,1)S(1)}, u32[]{:S(2)}, u32[]{:S(2)}) collective-permute-start(bf16[512,512]{0,1:T(8,128)(2,1)S(1)} %collective-permute-done), channel_id=1, source_target_pairs={{0,1},{1,2},{2,3},{3,4},{4,5},{5,6},{6,7},{7,8},{8,9},{9,10},{10,1... | collective-permute-start | bytes 1572872 | tf_op jit(solution)/shard_map/ppermute | solution.py:66
  91.2 15.2 %collective-permute-start.2 = (bf16[512,512]{0,1:T(8,128)(2,1)S(1)}, bf16[512,512]{0,1:T(8,128)(2,1)S(1)}, u32[]{:S(2)}, u32[]{:S(2)}) collective-permute-start(bf16[512,512]{0,1:T(8,128)(2,1)S(1)} %collective-permute-done.1), channel_id=1, source_target_pairs={{0,1},{1,2},{2,3},{3,4},{4,5},{5,6},{6,7},{7,8},{8,9},{9,10},{10,1... | collective-permute-start | bytes 1572872 | tf_op jit(solution)/shard_map/ppermute | solution.py:66
  106.4 14.3 %collective-permute-start.3 = (bf16[512,512]{0,1:T(8,128)(2,1)S(1)}, bf16[512,512]{0,1:T(8,128)(2,1)S(1)}, u32[]{:S(2)}, u32[]{:S(2)}) collective-permute-start(bf16[512,512]{0,1:T(8,128)(2,1)S(1)} %collective-permute-done.2), channel_id=1, source_target_pairs={{0,1},{1,2},{2,3},{3,4},{4,5},{5,6},{6,7},{7,8},{8,9},{9,10},{10,1... | collective-permute-start | bytes 1572872 | tf_op jit(solution)/shard_map/ppermute | solution.py:66
  120.7 13.4 %collective-permute-start.4 = (bf16[512,512]{0,1:T(8,128)(2,1)S(1)}, bf16[512,512]{0,1:T(8,128)(2,1)S(1)}, u32[]{:S(2)}, u32[]{:S(2)}) collective-permute-start(bf16[512,512]{0,1:T(8,128)(2,1)S(1)} %collective-permute-done.3), channel_id=1, source_target_pairs={{0,1},{1,2},{2,3},{3,4},{4,5},{5,6},{6,7},{7,8},{8,9},{9,10},{10,1... | collective-permute-start | bytes 1572872 | tf_op jit(solution)/shard_map/ppermute | solution.py:66
  134.1 12.5 %collective-permute-start.5 = (bf16[512,512]{0,1:T(8,128)(2,1)S(1)}, bf16[512,512]{0,1:T(8,128)(2,1)S(1)}, u32[]{:S(2)}, u32[]{:S(2)}) collective-permute-start(bf16[512,512]{0,1:T(8,128)(2,1)S(1)} %collective-permute-done.4), channel_id=1, source_target_pairs={{0,1},{1,2},{2,3},{3,4},{4,5},{5,6},{6,7},{7,8},{8,9},{9,10},{10,1... | collective-permute-start | bytes 1572872 | tf_op jit(solution)/shard_map/ppermute | solution.py:66
  147.4 11.5 %collective-permute-start.6 = (bf16[512,512]{0,1:T(8,128)(2,1)S(1)}, bf16[512,512]{0,1:T(8,128)(2,1)S(1)}, u32[]{:S(2)}, u32[]{:S(2)}) collective-permute-start(bf16[512,512]{0,1:T(8,128)(2,1)S(1)} %collective-permute-done.5), channel_id=1, source_target_pairs={{0,1},{1,2},{2,3},{3,4},{4,5},{5,6},{6,7},{7,8},{8,9},{9,10},{10,1... | collective-permute-start | bytes 1572872 | tf_op jit(solution)/shard_map/ppermute | solution.py:66
  158.9 0.8 copy-start.4
  159.7 12.2 %collective-permute-start.7 = (bf16[512,512]{0,1:T(8,128)(2,1)S(1)}, bf16[512,512]{0,1:T(8,128)(2,1)S(1)}, u32[]{:S(2)}, u32[]{:S(2)}) collective-permute-start(bf16[512,512]{0,1:T(8,128)(2,1)S(1)} %collective-permute-done.6), channel_id=1, source_target_pairs={{0,1},{1,2},{2,3},{3,4},{4,5},{5,6},{6,7},{7,8},{8,9},{9,10},{10,1... | collective-permute-start | bytes 1572872 | tf_op jit(solution)/shard_map/ppermute | solution.py:66
  171.9 0.8 copy-start.6
  172.7 13.3 %collective-permute-start.8 = (bf16[512,512]{0,1:T(8,128)(2,1)S(1)}, bf16[512,512]{0,1:T(8,128)(2,1)S(1)}, u32[]{:S(2)}, u32[]{:S(2)}) collective-permute-start(bf16[512,512]{0,1:T(8,128)(2,1)S(1)} %collective-permute-done.7), channel_id=1, source_target_pairs={{0,1},{1,2},{2,3},{3,4},{4,5},{5,6},{6,7},{7,8},{8,9},{9,10},{10,1... | collective-permute-start | bytes 1572872 | tf_op jit(solution)/shard_map/ppermute | solution.py:66
  186.8 14.3 %collective-permute-start.9 = (bf16[512,512]{0,1:T(8,128)(2,1)S(1)}, bf16[512,512]{0,1:T(8,128)(2,1)S(1)}, u32[]{:S(2)}, u32[]{:S(2)}) collective-permute-start(bf16[512,512]{0,1:T(8,128)(2,1)S(1)} %collective-permute-done.8), channel_id=1, source_target_pairs={{0,1},{1,2},{2,3},{3,4},{4,5},{5,6},{6,7},{7,8},{8,9},{9,10},{10,1... | collective-permute-start | bytes 1572872 | tf_op jit(solution)/shard_map/ppermute | solution.py:66
  202.0 15.5 %collective-permute-start.10 = (bf16[512,512]{0,1:T(8,128)(2,1)S(1)}, bf16[512,512]{0,1:T(8,128)(2,1)S(1)}, u32[]{:S(2)}, u32[]{:S(2)}) collective-permute-start(bf16[512,512]{0,1:T(8,128)(2,1)S(1)} %collective-permute-done.9), channel_id=1, source_target_pairs={{0,1},{1,2},{2,3},{3,4},{4,5},{5,6},{6,7},{7,8},{8,9},{9,10},{10,1... | collective-permute-start | bytes 1572872 | tf_op jit(solution)/shard_map/ppermute | solution.py:66
  218.2 16.6 %collective-permute-start.11 = (bf16[512,512]{0,1:T(8,128)(2,1)S(1)}, bf16[512,512]{0,1:T(8,128)(2,1)S(1)}, u32[]{:S(2)}, u32[]{:S(2)}) collective-permute-start(bf16[512,512]{0,1:T(8,128)(2,1)S(1)} %collective-permute-done.10), channel_id=1, source_target_pairs={{0,1},{1,2},{2,3},{3,4},{4,5},{5,6},{6,7},{7,8},{8,9},{9,10},{10,1... | collective-permute-start | bytes 1572872 | tf_op jit(solution)/shard_map/ppermute | solution.py:66
  235.6 15.7 %collective-permute-start.12 = (bf16[512,512]{0,1:T(8,128)(2,1)S(1)}, bf16[512,512]{0,1:T(8,128)(2,1)}, u32[]{:S(2)}, u32[]{:S(2)}) collective-permute-start(bf16[512,512]{0,1:T(8,128)(2,1)S(1)} %collective-permute-done.11), channel_id=1, source_target_pairs={{0,1},{1,2},{2,3},{3,4},{4,5},{5,6},{6,7},{7,8},{8,9},{9,10},{10,1... | collective-permute-start | bytes 1572872 | tf_op jit(solution)/shard_map/ppermute | solution.py:66
  251.3 15.0 %collective-permute-start.13 = (bf16[512,512]{0,1:T(8,128)(2,1)}, bf16[512,512]{0,1:T(8,128)(2,1)}, u32[]{:S(2)}, u32[]{:S(2)}) collective-permute-start(bf16[512,512]{0,1:T(8,128)(2,1)} %collective-permute-done.12), channel_id=1, source_target_pairs={{0,1},{1,2},{2,3},{3,4},{4,5},{5,6},{6,7},{7,8},{8,9},{9,10},{10,1... | collective-permute-start | bytes 1572872 | tf_op jit(solution)/shard_map/ppermute | solution.py:66
  251.5 38.6 %copy-start.15 = (bf16[512,512]{0,1:T(8,128)(2,1)S(1)}, bf16[512,512]{0,1:T(8,128)(2,1)}, u32[]{:S(2)}) copy-start(bf16[512,512]{0,1:T(8,128)(2,1)} %copy-done.14) | copy-start | bytes 1572868
  251.5 38.7 %copy-start.13 = (bf16[512,512]{0,1:T(8,128)(2,1)S(1)}, bf16[512,512]{0,1:T(8,128)(2,1)}, u32[]{:S(2)}) copy-start(bf16[512,512]{0,1:T(8,128)(2,1)} %copy-done.12) | copy-start | bytes 1572868
  251.5 38.7 %copy-start.11 = (bf16[512,512]{0,1:T(8,128)(2,1)S(1)}, bf16[512,512]{0,1:T(8,128)(2,1)}, u32[]{:S(2)}) copy-start(bf16[512,512]{0,1:T(8,128)(2,1)} %copy-done.10) | copy-start | bytes 1572868
  251.5 38.7 %copy-start.9 = (bf16[512,512]{0,1:T(8,128)(2,1)S(1)}, bf16[512,512]{0,1:T(8,128)(2,1)}, u32[]{:S(2)}) copy-start(bf16[512,512]{0,1:T(8,128)(2,1)} %copy-done.8) | copy-start | bytes 1572868
  251.5 38.8 %copy-start.7 = (bf16[512,512]{0,1:T(8,128)(2,1)S(1)}, bf16[512,512]{0,1:T(8,128)(2,1)}, u32[]{:S(2)}) copy-start(bf16[512,512]{0,1:T(8,128)(2,1)} %copy-done.6) | copy-start | bytes 1572868
  251.5 38.8 %copy-start.5 = (bf16[512,512]{0,1:T(8,128)(2,1)S(1)}, bf16[512,512]{0,1:T(8,128)(2,1)}, u32[]{:S(2)}) copy-start(bf16[512,512]{0,1:T(8,128)(2,1)} %copy-done.4) | copy-start | bytes 1572868
  251.5 38.9 %copy-start.3 = (bf16[512,512]{0,1:T(8,128)(2,1)S(1)}, bf16[512,512]{0,1:T(8,128)(2,1)}, u32[]{:S(2)}) copy-start(bf16[512,512]{0,1:T(8,128)(2,1)} %copy-done.2) | copy-start | bytes 1572868
  266.3 11.5 %collective-permute-start.14 = (bf16[512,512]{0,1:T(8,128)(2,1)}, bf16[512,512]{0,1:T(8,128)(2,1)S(1)}, u32[]{:S(2)}, u32[]{:S(2)}) collective-permute-start(bf16[512,512]{0,1:T(8,128)(2,1)} %collective-permute-done.13), channel_id=1, source_target_pairs={{0,1},{1,2},{2,3},{3,4},{4,5},{5,6},{6,7},{7,8},{8,9},{9,10},{10,1... | collective-permute-start | bytes 1572872 | tf_op jit(solution)/shard_map/ppermute | solution.py:66
  285.4 7.1 %copy-start.16 = (f32[8192]{0:T(1024)S(1)}, f32[8192]{0:T(1024)}, u32[]{:S(2)}) copy-start(f32[8192]{0:T(1024)} %param.17) | copy-start | bytes 98308
  350.3 196.9 %copy-start.1 = (bf16[512,512]{1,0:T(8,128)(2,1)S(1)}, bf16[512,512]{1,0:T(8,128)(2,1)}, u32[]{:S(2)}) copy-start(bf16[512,512]{1,0:T(8,128)(2,1)} %param.14) | copy-start | bytes 1572868
  (5 other events, 4.0 us)
Sparse Core Ops, SparseCore 0:
  9.5 42.6 all-gather.2
  433.3 111.2 reduce-scatter.1
